TPU v7x, 128 devices: a whole 4x4x4 slice. The times are simulated.
128 devices in a mesh: section: 16 (over z, y_lo, core), tensor: 8 (over y_hi, x).
Axes of the slice: x: 4, y: 4 (y_hi: 2, y_lo: 2; y = y_hi * 2 + y_lo), z: 4, core: 2. Of those that a mesh axis runs over, the one named last changes fastest.
Arguments:
- token_ids: int32 [4096], P('section'), may hold values from 0 to 152063, as said below
- column_order: int32 [8192], replicated, may hold values from 0 to 8191, each once
- residual: bfloat16 [4096, 8192], P('section', 'tensor'), may hold values from -40 to 40
- attn_out: bfloat16 [4096, 8192], P('section', 'tensor'), may hold values from -6 to 6
- out_proj: bfloat16 [8192, 8192], P(None, 'tensor'), may hold values from -0.0625 to 0.0625
- norm_gain: float32 [8192], P('tensor'), may hold values from 0.5 to 1.5
Outputs:
- factored: float32 [8192, 8192], P('section', 'tensor')
Inputs may be any that keep to these rules, and one draw needn't show every extreme that they name: `token_ids`: id 0 marks padding. In each block of 256 tokens of one section index the padding fills trailing positions, and each block holds at least one non-padding token.
All inputs are finite; a program needn't handle non-finite values.
Results may differ from a plain program's by a relative error of at most 0.0067.
Values may be sent and summed in bfloat16 or wider, within the bound.
No kernel may reach another device: no remote copies, remote signals or barrier semaphores. Data moves between devices by JAX's collectives and lax.ppermute only.
A program may use at most 128 MiB of HBM per device.

v0:
```python
import jax
import jax.numpy as jnp
from jax import lax
from jax.sharding import PartitionSpec as P

TILE = 128
PANEL = 1024
epsilon = 1e-06


def spread(value, axis, source):
    kept = jnp.where(lax.axis_index(axis) == source, value, 0).astype(value.dtype)
    return lax.psum(kept, axis)


def shards(token_ids, column_order, residual, attn_out, out_proj, norm_gain):
    section_count = lax.axis_size("section")
    tensor_count = lax.axis_size("tensor")
    section_id = lax.axis_index("section")
    tensor_id = lax.axis_index("tensor")
    model_width = out_proj.shape[0]
    span_rows = model_width // section_count
    span_cols = model_width // tensor_count
    projected = jnp.dot(
        lax.all_gather(attn_out, "tensor", axis=1, tiled=True),
        out_proj,
        preferred_element_type=jnp.float32,
    )
    rounded = (residual.astype(jnp.float32) + projected).astype(jnp.bfloat16)
    hidden = lax.optimization_barrier(rounded).astype(jnp.float32)
    squares = lax.psum(jnp.sum(hidden * hidden, axis=1), "tensor")
    kept_rows = (token_ids != 0).astype(jnp.float32)
    token_count = lax.psum(jnp.sum(kept_rows), "section")
    row_scale = lax.rsqrt(squares / model_width + epsilon) * kept_rows
    normed = (hidden * row_scale[:, None] * norm_gain[None, :]).astype(jnp.bfloat16)
    target = jnp.arange(section_count, dtype=jnp.int32)[:, None, None]
    tile_index = jnp.arange(span_rows // TILE, dtype=jnp.int32)[None, :, None]
    offset = jnp.arange(TILE, dtype=jnp.int32)[None, None, :]
    send_global = ((tile_index * section_count + target) * TILE + offset).reshape(model_width)
    col_tiles = jnp.arange(span_cols // TILE, dtype=jnp.int32)[:, None]
    cols_global = (
        (col_tiles * tensor_count + tensor_id) * TILE + jnp.arange(TILE, dtype=jnp.int32)[None, :]
    ).reshape(span_cols)
    full_rows = lax.all_gather(normed, "tensor", axis=1, tiled=True)
    outgoing = jnp.take(full_rows, jnp.take(column_order, send_global), axis=1)
    mine_rows = lax.all_to_all(outgoing, "section", split_axis=1, concat_axis=0, tiled=True)
    col_part = jnp.take(full_rows, jnp.take(column_order, cols_global), axis=1)
    gram_sum = lax.dot_general(
        mine_rows,
        lax.all_gather(col_part, "section", axis=0, tiled=True),
        (((0,), (0,)), ((), ())),
        preferred_element_type=jnp.float32,
    )
    hessian = gram_sum / token_count
    panel_local = PANEL // tensor_count
    per_group = panel_local // TILE
    gathered = lax.all_gather(hessian[:, :panel_local], "tensor", axis=1, tiled=True)
    panel_rows = (
        gathered.reshape(span_rows, tensor_count, per_group, TILE)
        .transpose(0, 2, 1, 3)
        .reshape(span_rows, PANEL)
    )
    first_tile = panel_rows[:TILE]
    stacked = lax.all_gather(first_tile, "section", axis=0, tiled=True)
    diag_block = stacked[:PANEL]
    chol_low = jnp.linalg.cholesky(diag_block)
    own_lower = lax.linalg.triangular_solve(
        chol_low, panel_rows, left_side=False, lower=True, transpose_a=True
    )
    copies = [
        spread(own_lower, "section", tensor_id + second * tensor_count)
        for second in range(section_count // tensor_count)
    ]
    shaped = [copy_rows.reshape(span_rows // TILE, TILE, PANEL) for copy_rows in copies]
    other_lower = jnp.stack(shaped, axis=1).reshape(span_cols, PANEL)
    row_tiles = jnp.arange(span_rows // TILE, dtype=jnp.int32)[:, None]
    rows_global = (
        (row_tiles * section_count + section_id) * TILE + jnp.arange(TILE, dtype=jnp.int32)[None, :]
    ).reshape(span_rows)
    panel_global = cols_global[:panel_local]
    left_part = jnp.take(own_lower, panel_global, axis=1)
    left_part = jnp.where(
        rows_global[:, None] >= panel_global[None, :], left_part, jnp.float32(0.0)
    )
    update = jnp.dot(
        own_lower,
        other_lower[panel_local:].T,
        precision=lax.Precision.HIGHEST,
        preferred_element_type=jnp.float32,
    )
    right_part = hessian[:, panel_local:] - update
    return jnp.concatenate([left_part, right_part], axis=1)


def solution(mesh):
    placed = (
        P("section"),
        P(),
        P("section", "tensor"),
        P("section", "tensor"),
        P(None, "tensor"),
        P("tensor"),
    )
    return jax.shard_map(
        shards, mesh=mesh, in_specs=placed, out_specs=P("section", "tensor"), check_vma=False
    )
```

profile of v0, /device:TPU:0, one launch (start us, length us, event | category | flops | bytes accessed | tf_op | source)
XLA Modules:
  0.0 999.8 jit_solution(9918803187925176559)
XLA Ops:
  7.3 76.3 %all-gather.6.cloned.1.call-done = bf16[256,8192]{1,0:T(8,128)(2,1)} async-done(((bf16[256,1024]{1,0:T(8,128)(2,1)}), bf16[256,8192]{1,0:T(8,128)(2,1)}) %all-gather.6.cloned.1.call-update) | async-done | bytes 4194320 | tf_op jit(solution)/shard_map/all_gather | solution.py:25
  83.7 11.5 %fusion.5 = bf16[256,1024]{1,0:T(8,128)(2,1)S(1)} fusion(bf16[256,8192]{1,0:T(8,128)(2,1)} %all-gather.6.cloned.1.call-done, bf16[8192,1024]{1,0:T(8,128)(2,1)} %param.10, bf16[256,1024]{1,0:T(8,128)(2,1)} %param.8), kind=kOutput, calls=%fused_computation.21 | convolution fusion | flops 4295753728 | bytes 22020096 | tf_op jit(solution)/shard_map/dot_general | solution.py:24
  95.3 19.8 %psum.28 = f32[256]{0:T(256)S(1)} all-reduce(f32[256]{0:T(256)S(1)} %fusion.6), channel_id=1, replica_groups=mesh['section'=16,'tensor'=8] {'tensor'}, use_global_device_ids=true, to_apply=%region_1.0 | all-reduce | flops 256 | bytes 2048 | tf_op jit(solution)/shard_map/psum | solution.py:31
  117.0 6.2 gather_fusion.2
  123.2 64.0 %all-gather.8.cloned.1.call-done = bf16[256,8192]{1,0:T(8,128)(2,1)} async-done(((bf16[256,1024]{1,0:T(8,128)(2,1)}), bf16[256,8192]{1,0:T(8,128)(2,1)}) %all-gather.8.cloned.1.call-update) | async-done | bytes 4194320 | tf_op jit(solution)/shard_map/all_gather | solution.py:44
  187.3 6.4 copy.13
  193.6 6.2 gather_fusion.3
  201.0 45.5 %gather_fusion = s32[8192]{0:T(1024)S(1)} fusion(s32[8192]{0:T(1024)S(1)} %copy-done, s32[8192]{0:T(1024)S(1)} %broadcast_clamp_fusion.1), kind=kCustom, calls=%fused_computation | custom fusion | bytes 98304 | tf_op jit(solution)/shard_map/jit(_take)/gather | solution.py:45
  246.7 33.9 %gather_fusion.1 = bf16[8192,256]{1,0:T(8,128)(2,1)} fusion(bf16[256,8192]{0,1:T(8,128)(2,1)} %copy.13, s32[8192]{0:T(1024)S(1)} %broadcast_clamp_fusion), kind=kCustom, calls=%fused_computation.1 | custom fusion | bytes 8421376 | tf_op jit(solution)/shard_map/jit(_take)/gather | solution.py:45
  280.6 6.4 copy.14
  287.0 4.6 broadcast_select_fusion
  291.6 4.6 all-to-all-start
  296.2 72.6 %psum.29 = f32[]{:T(128)} all-reduce(f32[]{:T(128)} %get-tuple-element.74), channel_id=1, replica_groups=mesh['section'=16,'tensor'=8] {'section'}, use_global_device_ids=true, to_apply=%region_3.0 | all-reduce | flops 1 | bytes 8 | tf_op jit(solution)/shard_map/psum | solution.py:33
  368.9 8.8 convolution_divide_fusion
  379.8 51.4 %all-gather.12.cloned.1.call-done = f32[512,1024]{0,1:T(8,128)} async-done(((f32[512,128]{0,1:T(8,128)}), f32[512,1024]{0,1:T(8,128)}) %all-gather.12.cloned.1.call-update) | async-done | bytes 2097168 | tf_op jit(solution)/shard_map/all_gather | solution.py:57
  433.3 59.7 %all-gather.14.cloned.1.call-done = f32[2048,1024]{0,1:T(8,128)} async-done(((f32[128,1024]{0,1:T(8,128)}), f32[2048,1024]{0,1:T(8,128)}) %all-gather.14.cloned.1.call-update) | async-done | bytes 8388624 | tf_op jit(solution)/shard_map/all_gather | solution.py:64
  493.0 4.7 slice.274
  497.8 5.5 copy.17
  503.2 4.4 fusion
  509.7 11.7 %cholesky.223 = f32[128,128]{1,0:T(8,128)S(1)} custom-call(f32[128,128]{1,0:T(8,128)S(1)} %cholesky.580), custom_call_target="Cholesky" | custom-call | tf_op jit(solution)/shard_map/jit(cholesky)/cholesky | solution.py:66
  521.5 9.8 custom-call.62
  531.3 2.6 cholesky.255
  533.8 2.4 constant_dynamic-update-slice_fusion.32
  537.8 11.9 %cholesky.244 = f32[128,128]{1,0:T(8,128)S(1)} custom-call(f32[128,128]{1,0:T(8,128)S(1)} %cholesky.584), custom_call_target="Cholesky" | custom-call | tf_op jit(solution)/shard_map/jit(cholesky)/cholesky | solution.py:66
  550.3 9.8 custom-call.63
  563.5 11.7 %cholesky.468 = f32[128,128]{1,0:T(8,128)S(1)} custom-call(f32[128,128]{1,0:T(8,128)S(1)} %cholesky.589), custom_call_target="Cholesky" | custom-call | tf_op jit(solution)/shard_map/jit(cholesky)/cholesky | solution.py:66
  576.5 9.8 custom-call.64
  587.5 2.3 convolution_subtract_fusion.2
  589.8 12.1 %cholesky.487 = f32[128,128]{1,0:T(8,128)S(1)} custom-call(f32[128,128]{1,0:T(8,128)S(1)} %cholesky.594), custom_call_target="Cholesky" | custom-call | tf_op jit(solution)/shard_map/jit(cholesky)/cholesky | solution.py:66
  603.2 9.8 custom-call.65
  614.1 2.3 convolution_subtract_fusion.10
  616.5 11.7 %cholesky.506 = f32[128,128]{1,0:T(8,128)S(1)} custom-call(f32[128,128]{1,0:T(8,128)S(1)} %cholesky.599), custom_call_target="Cholesky" | custom-call | tf_op jit(solution)/shard_map/jit(cholesky)/cholesky | solution.py:66
  629.5 9.9 custom-call.66
  640.5 2.3 convolution_subtract_fusion.11
  642.7 11.7 %cholesky.526 = f32[128,128]{1,0:T(8,128)S(1)} custom-call(f32[128,128]{1,0:T(8,128)S(1)} %cholesky.604), custom_call_target="Cholesky" | custom-call | tf_op jit(solution)/shard_map/jit(cholesky)/cholesky | solution.py:66
  655.8 9.8 custom-call.67
  668.6 11.9 %cholesky.546 = f32[128,128]{1,0:T(8,128)S(1)} custom-call(f32[128,128]{1,0:T(8,128)S(1)} %cholesky.609), custom_call_target="Cholesky" | custom-call | tf_op jit(solution)/shard_map/jit(cholesky)/cholesky | solution.py:66
  681.8 9.8 custom-call.68
  694.3 11.7 %cholesky.564 = f32[128,128]{1,0:T(8,128)S(1)} custom-call(f32[128,128]{1,0:T(8,128)S(1)} %convolution_subtract_fusion.13), custom_call_target="Cholesky" | custom-call | tf_op jit(solution)/shard_map/jit(cholesky)/cholesky | solution.py:66
  712.9 4.9 select_select_fusion
  717.8 22.9 %while.1 = (s32[]{:T(128)}, f32[1024,1024]{1,0:T(8,128)}, s32[8,2]{0,1:T(2,128)S(1)}, f32[8,128,128]{2,1,0:T(8,128)S(1)}, s32[]{:T(128)}) while((s32[]{:T(128)}, f32[1024,1024]{1,0:T(8,128)}, s32[8,2]{0,1:T(2,128)S(1)}, f32[8,128,128]{2,1,0:T(8,128)S(1)}, s32[]{:T(128)}) %tuple.59), condition=%wide.while_cond, body=%wide.while_body.sunk | while | flops 2 | bytes 131181 | solution.py:67
  740.7 79.0 %custom-call.69 = f32[8,128,128]{1,2,0:T(8,128)S(1)} custom-call(f32[8,128,128]{2,1,0:T(8,128)S(1)} %get-tuple-element.12), custom_call_target="InvertDiagBlocksLowerTriangular" | custom-call | tf_op jit(solution)/shard_map/triangular_solve | solution.py:67
  836.8 2.7 broadcast_select_fusion.2
  839.5 2.9 copy.24
  842.5 3.0 copy.25
  846.5 135.4 %all-reduce.4.cloned.1.call-done = (f32[4,1,128,1024]{3,2,1,0:T(8,128)}, f32[4,1,128,1024]{3,2,1,0:T(8,128)}) async-done(((f32[4,1,128,1024]{3,2,1,0:T(8,128)}, f32[4,1,128,1024]{3,2,1,0:T(8,128)}), (f32[4,1,128,1024]{3,2,1,0:T(8,128)}, f32[4,1,128,1024]{3,2,1,0:T(8,128)})) %all-reduce.4.cloned.1.call-update) | async-done | bytes 4194320 | tf_op jit(solution)/shard_map/psum | solution.py:13
  981.9 2.7 pad_maximum_fusion
  984.8 6.0 slice_subtract_fusion
  (136 shorter events, 76.3 us)
Async XLA Ops:
  6.5 110.4 %copy-start = (s32[8192]{0:T(1024)S(1)}, s32[8192]{0:T(1024)}, u32[]{:S(2)}) copy-start(s32[8192]{0:T(1024)} %param.7) | copy-start | bytes 98308
  6.5 77.1 %all-gather.6.cloned.1.call-start = ((), (), s32[]{:S(2)}) async-start(), calls=%async_computation.1 | async-start | bytes 4718592 | tf_op jit(solution)/shard_map/all_gather | solution.py:25
  7.3 107.8 %copy-start.7 = (s32[256]{0:T(256)S(1)}, s32[256]{0:T(256)}, u32[]{:S(2)}) copy-start(s32[256]{0:T(256)} %param.6) | copy-start | bytes 3076
  7.3 108.5 %copy-start.6 = (f32[1024]{0:T(1024)S(1)}, f32[1024]{0:T(1024)}, u32[]{:S(2)}) copy-start(f32[1024]{0:T(1024)} %param.11) | copy-start | bytes 12292
  7.3 180.0 %all-gather.8.cloned.1.call-start = ((), (), s32[]{:S(2)}) async-start(), calls=%async_computation.2 | async-start | bytes 4718592 | tf_op jit(solution)/shard_map/all_gather | solution.py:44
  116.8 252.1 %all-gather.10.cloned.1.call-start = ((), (), s32[]{:S(2)}) async-start(), calls=%async_computation.3 | async-start | bytes 8912896 | tf_op jit(solution)/shard_map/all_gather | solution.py:50
  291.6 77.3 %all-to-all-start = ((bf16[256,16,512]{2,0,1:T(8,128)(2,1)}), bf16[256,16,512]{2,0,1:T(8,128)(2,1)}, u32[]{:S(2)}, u32[]{:S(2)}) async-start(bf16[256,16,512]{2,0,1:T(8,128)(2,1)} %broadcast_select_fusion), calls=%async_computation | async-start | bytes 8388608 | tf_op jit(solution)/shard_map/all_to_all | solution.py:46
  296.2 135.1 %all-gather.12.cloned.1.call-start = ((), (), s32[]{:S(2)}) async-start(), calls=%async_computation.4 | async-start | bytes 2359296 | tf_op jit(solution)/shard_map/all_gather | solution.py:57
  377.7 1.3 copy-start.3
  379.8 113.2 %all-gather.14.cloned.1.call-start = ((), (), s32[]{:S(2)}) async-start(), calls=%async_computation.5 | async-start | bytes 8912896 | tf_op jit(solution)/shard_map/all_gather | solution.py:64
  433.2 548.8 %all-reduce.4.cloned.1.call-start = ((), (), s32[]{:S(2)}) async-start(), calls=%async_computation.6 | async-start | bytes 8388608 | tf_op jit(solution)/shard_map/psum | solution.py:13
  507.7 2.0 copy-start.2
  821.1 6.1 copy-start.5
  981.9 2.9 copy-start.4
  984.8 8.0 copy-start.1
Sparse Core Ops, SparseCore 0:
  9.7 73.9 all-gather.5
  116.9 70.3 all-gather.7
  201.0 58.7 all-gather.9
  379.9 51.3 all-gather.11
  433.3 59.6 all-gather.13
  845.7 136.2 all-reduce.3
where the time goes:
time: 1010 us; the launch traced here: 1000 us
  waiting for transfers between devices  388 us (38%)
  other arithmetic  274 us (27%)
  local copies, waits for them, and re-layouts  155 us (15%)
  blocking collectives  92.4 us (9%)
  matrix products  66.5 us (7%)
  between operations  19.2 us (2%)
    another operation x30, other arithmetic, shards(): chol_low = jnp.linalg.cholesky(diag_block)  172 us
    psum x1, waiting for transfers between devices, spread(): return lax.psum(kept, axis)  135 us
    gather x4, local copies, waits for them, and re-layouts, shards(): outgoing = jnp.take(full_rows, jnp.take(column_order, send_global), axis=1)  85.8 us
    another operation x3, other arithmetic, shards(): lax.linalg.triangular_solve(chol_low, panel_rows, left_side=False, lower=...  83.9 us
    all_gather x1, waiting for transfers between devices, shards(): lax.all_gather(attn_out, 'tensor', axis=1, tiled=True)  76.3 us
    psum x1, blocking collectives, shards(): token_count = lax.psum(jnp.sum(kept_rows), 'section')  72.6 us
    all_gather x1, waiting for transfers between devices, shards(): full_rows = lax.all_gather(normed, 'tensor', axis=1, tiled=True)  64 us
    all_gather x1, waiting for transfers between devices, shards(): stacked = lax.all_gather(first_tile, 'section', axis=0, tiled=True)  59.7 us
  transfers between devices with their start and end apart: 7, of which 5 were waited for; matrix products, arithmetic and copies ran while one was open for 10% of the time, Pallas kernels for 0%

commit v1 on v0

--- a/solution.py
+++ b/solution.py
@@ -10,7 +10,11 @@
 
 def spread(value, axis, source):
     kept = jnp.where(lax.axis_index(axis) == source, value, 0).astype(value.dtype)
-    return lax.psum(kept, axis)
+
+    def search_surface_for(own_rows):
+        return jnp.sum(lax.all_gather(own_rows, axis_name=axis), 0)
+
+    return search_surface_for(kept)
 
 
 def shards(token_ids, column_order, residual, attn_out, out_proj, norm_gain):

time: 1010 us -> 1230 us (1.22)
  waiting for transfers between devices: 388 us -> 578 us
  other arithmetic: 274 us -> 301 us
    all_gather x0 -> x2, waiting for transfers between devices: none -> 326 us  [search_surface_for(): return jnp.sum(lax.all_gather(own_rows, axis_name=axis), 0)]
    psum x1 -> x0, waiting for transfers between devices: 135 us -> none  [spread(): return lax.psum(kept, axis)]
    reduce_sum x0 -> x2, other arithmetic: none -> 26.8 us  [search_surface_for(): return jnp.sum(lax.all_gather(own_rows, axis_name=axis), 0)]
    another operation x26 -> x24, local copies, waits for them, and re-layouts: 28.7 us -> 22.7 us
    another operation x30 -> x31, other arithmetic: 172 us -> 173 us  [shards(): chol_low = jnp.linalg.cholesky(diag_block)]
  transfers between devices with their start and end apart: 7 -> 8, of which waited for: 5 -> 6; matrix products, arithmetic and copies ran while one was open for 10% -> 9% of each run, Pallas kernels for 0% -> 0%
where the time goes in v1:
time: 1230 us; the launch traced here: 1220 us
  waiting for transfers between devices  578 us (47%)
  other arithmetic  301 us (24%)
  local copies, waits for them, and re-layouts  155 us (13%)
  blocking collectives  92.3 us (8%)
  matrix products  66.1 us (5%)
  between operations  19.3 us (2%)
    all_gather x2, waiting for transfers between devices, search_surface_for(): return jnp.sum(lax.all_gather(own_rows, axis_name=axis), 0)  326 us
    another operation x31, other arithmetic, shards(): chol_low = jnp.linalg.cholesky(diag_block)  173 us
    gather x4, local copies, waits for them, and re-layouts, shards(): outgoing = jnp.take(full_rows, jnp.take(column_order, send_global), axis=1)  85.7 us
    another operation x3, other arithmetic, shards(): lax.linalg.triangular_solve(chol_low, panel_rows, left_side=False, lower=...  83.8 us
    all_gather x1, waiting for transfers between devices, shards(): lax.all_gather(attn_out, 'tensor', axis=1, tiled=True)  76.3 us
    psum x1, blocking collectives, shards(): token_count = lax.psum(jnp.sum(kept_rows), 'section')  72.6 us
    all_gather x1, waiting for transfers between devices, shards(): full_rows = lax.all_gather(normed, 'tensor', axis=1, tiled=True)  64 us
    all_gather x1, waiting for transfers between devices, shards(): stacked = lax.all_gather(first_tile, 'section', axis=0, tiled=True)  59.7 us
  transfers between devices with their start and end apart: 8, of which 6 were waited for; matrix products, arithmetic and copies ran while one was open for 9% of the time, Pallas kernels for 0%

profile of v1, /device:TPU:0, one launch (start us, length us, event | category | flops | bytes accessed | tf_op | source)
XLA Modules:
  0.0 1217.0 jit_solution(15423206846366307207)
XLA Ops:
  7.3 76.3 %all-gather.8.cloned.1.call-done = bf16[256,8192]{1,0:T(8,128)(2,1)} async-done(((bf16[256,1024]{1,0:T(8,128)(2,1)}), bf16[256,8192]{1,0:T(8,128)(2,1)}) %all-gather.8.cloned.1.call-update) | async-done | bytes 4194320 | tf_op jit(solution)/shard_map/all_gather | solution.py:29
  83.7 11.5 fusion.5
  95.3 19.8 %psum.14 = f32[256]{0:T(256)S(1)} all-reduce(f32[256]{0:T(256)S(1)} %fusion.6), channel_id=1, replica_groups=mesh['section'=16,'tensor'=8] {'tensor'}, use_global_device_ids=true, to_apply=%region_1.0 | all-reduce | flops 256 | bytes 2048 | tf_op jit(solution)/shard_map/psum | solution.py:35
  116.9 6.2 gather_fusion.2
  123.2 64.0 %all-gather.10.cloned.1.call-done = bf16[256,8192]{1,0:T(8,128)(2,1)} async-done(((bf16[256,1024]{1,0:T(8,128)(2,1)}), bf16[256,8192]{1,0:T(8,128)(2,1)}) %all-gather.10.cloned.1.call-update) | async-done | bytes 4194320 | tf_op jit(solution)/shard_map/all_gather | solution.py:48
  187.2 6.4 copy.20
  193.6 6.2 gather_fusion.3
  201.0 45.5 %gather_fusion = s32[8192]{0:T(1024)S(1)} fusion(s32[8192]{0:T(1024)S(1)} %copy-done, s32[8192]{0:T(1024)S(1)} %broadcast_clamp_fusion.1), kind=kCustom, calls=%fused_computation | custom fusion | bytes 98304 | tf_op jit(solution)/shard_map/jit(_take)/gather | solution.py:49
  246.7 33.7 %gather_fusion.1 = bf16[8192,256]{1,0:T(8,128)(2,1)} fusion(bf16[256,8192]{0,1:T(8,128)(2,1)} %copy.20, s32[8192]{0:T(1024)S(1)} %broadcast_clamp_fusion), kind=kCustom, calls=%fused_computation.1 | custom fusion | bytes 8421376 | tf_op jit(solution)/shard_map/jit(_take)/gather | solution.py:49
  280.4 6.4 copy.21
  286.8 4.5 broadcast_select_fusion
  291.3 4.6 all-to-all-start
  295.9 72.6 %psum.15 = f32[]{:T(128)} all-reduce(f32[]{:T(128)} %get-tuple-element.72), channel_id=1, replica_groups=mesh['section'=16,'tensor'=8] {'section'}, use_global_device_ids=true, to_apply=%region_3.0 | all-reduce | flops 1 | bytes 8 | tf_op jit(solution)/shard_map/psum | solution.py:37
  368.5 8.8 convolution_divide_fusion
  379.4 51.4 %all-gather.14.cloned.1.call-done = f32[512,1024]{0,1:T(8,128)} async-done(((f32[512,128]{0,1:T(8,128)}), f32[512,1024]{0,1:T(8,128)}) %all-gather.14.cloned.1.call-update) | async-done | bytes 2097168 | tf_op jit(solution)/shard_map/all_gather | solution.py:61
  432.8 59.7 %all-gather.16.cloned.1.call-done = f32[2048,1024]{0,1:T(8,128)} async-done(((f32[128,1024]{0,1:T(8,128)}), f32[2048,1024]{0,1:T(8,128)}) %all-gather.16.cloned.1.call-update) | async-done | bytes 8388624 | tf_op jit(solution)/shard_map/all_gather | solution.py:68
  492.6 4.7 slice.274
  497.3 5.5 copy.24
  502.8 4.4 fusion
  509.2 11.7 cholesky.223
  520.9 2.5 cholesky.255
  523.4 9.8 custom-call.62
  533.2 2.4 constant_dynamic-update-slice_fusion.33
  537.2 11.9 cholesky.244
  549.7 9.8 custom-call.63
  562.9 11.7 cholesky.468
  575.2 9.8 custom-call.64
  588.6 12.1 cholesky.487
  601.3 9.8 custom-call.65
  614.6 11.7 cholesky.506
  626.9 10.0 custom-call.66
  640.2 11.7 cholesky.526
  652.5 9.8 custom-call.67
  665.3 11.7 cholesky.546
  677.7 9.8 custom-call.68
  690.1 11.7 cholesky.564
  712.8 4.8 select_select_fusion
  717.6 22.8 %while.1 = (s32[]{:T(128)}, f32[1024,1024]{1,0:T(8,128)}, s32[8,2]{0,1:T(2,128)S(1)}, f32[8,128,128]{2,1,0:T(8,128)S(1)}, s32[]{:T(128)}) while((s32[]{:T(128)}, f32[1024,1024]{1,0:T(8,128)}, s32[8,2]{0,1:T(2,128)S(1)}, f32[8,128,128]{2,1,0:T(8,128)S(1)}, s32[]{:T(128)}) %tuple.63), condition=%wide.while_cond, body=%wide.while_body.sunk | while | flops 2 | bytes 131189 | solution.py:71
  740.5 79.0 %custom-call.69 = f32[8,128,128]{1,2,0:T(8,128)S(1)} custom-call(f32[8,128,128]{2,1,0:T(8,128)S(1)} %get-tuple-element.12), custom_call_target="InvertDiagBlocksLowerTriangular" | custom-call | tf_op jit(solution)/shard_map/triangular_solve | solution.py:71
  836.6 2.5 broadcast_select_fusion.2
  839.1 2.9 copy.34
  842.1 3.1 copy.32
  846.2 166.2 %all-gather.20.cloned.1.call-done = f32[16,512,1024]{2,1,0:T(8,128)} async-done(((f32[1,512,1024]{2,1,0:T(8,128)}), f32[16,512,1024]{2,1,0:T(8,128)}) %all-gather.20.cloned.1.call-update) | async-done | bytes 33554448 | tf_op jit(solution)/shard_map/all_gather | solution.py:15
  1012.3 13.4 %reduce_sum.39 = f32[512,1024]{1,0:T(8,128)} reduce(f32[16,512,1024]{2,1,0:T(8,128)} %all-gather.20.cloned.1.call-done, f32[]{:T(128)} %constant.356.clone.1), dimensions={0}, to_apply=%region_21.22 | reduce | flops 7864320 | bytes 35651588 | tf_op jit(solution)/shard_map/reduce_sum | solution.py:15
  1025.7 159.9 %all-gather.18.cloned.1.call-done = f32[16,512,1024]{2,1,0:T(8,128)} async-done(((f32[1,512,1024]{2,1,0:T(8,128)}), f32[16,512,1024]{2,1,0:T(8,128)}) %all-gather.18.cloned.1.call-update) | async-done | bytes 33554448 | tf_op jit(solution)/shard_map/all_gather | solution.py:15
  1185.7 13.4 %reduce_sum.38 = f32[512,1024]{1,0:T(8,128)} reduce(f32[16,512,1024]{2,1,0:T(8,128)} %all-gather.18.cloned.1.call-done, f32[]{:T(128)} %constant.356.clone.1), dimensions={0}, to_apply=%region_20.21 | reduce | flops 7864320 | bytes 35651588 | tf_op jit(solution)/shard_map/reduce_sum | solution.py:15
  1199.1 2.7 pad_maximum_fusion
  1201.9 6.0 slice_subtract_fusion
  (149 shorter events, 83.6 us)
Async XLA Ops:
  6.5 110.4 %copy-start = (s32[8192]{0:T(1024)S(1)}, s32[8192]{0:T(1024)}, u32[]{:S(2)}) copy-start(s32[8192]{0:T(1024)} %param.7) | copy-start | bytes 98308
  6.5 77.1 %all-gather.8.cloned.1.call-start = ((), (), s32[]{:S(2)}) async-start(), calls=%async_computation.1 | async-start | bytes 4718592 | tf_op jit(solution)/shard_map/all_gather | solution.py:29
  7.3 107.8 %copy-start.7 = (s32[256]{0:T(256)S(1)}, s32[256]{0:T(256)}, u32[]{:S(2)}) copy-start(s32[256]{0:T(256)} %param.6) | copy-start | bytes 3076
  7.3 108.5 %copy-start.6 = (f32[1024]{0:T(1024)S(1)}, f32[1024]{0:T(1024)}, u32[]{:S(2)}) copy-start(f32[1024]{0:T(1024)} %param.11) | copy-start | bytes 12292
  7.3 179.9 %all-gather.10.cloned.1.call-start = ((), (), s32[]{:S(2)}) async-start(), calls=%async_computation.2 | async-start | bytes 4718592 | tf_op jit(solution)/shard_map/all_gather | solution.py:48
  116.7 251.8 %all-gather.12.cloned.1.call-start = ((), (), s32[]{:S(2)}) async-start(), calls=%async_computation.3 | async-start | bytes 8912896 | tf_op jit(solution)/shard_map/all_gather | solution.py:54
  291.3 77.2 %all-to-all-start = ((bf16[256,16,512]{2,0,1:T(8,128)(2,1)}), bf16[256,16,512]{2,0,1:T(8,128)(2,1)}, u32[]{:S(2)}, u32[]{:S(2)}) async-start(bf16[256,16,512]{2,0,1:T(8,128)(2,1)} %broadcast_select_fusion), calls=%async_computation | async-start | bytes 8388608 | tf_op jit(solution)/shard_map/all_to_all | solution.py:50
  295.9 134.9 %all-gather.14.cloned.1.call-start = ((), (), s32[]{:S(2)}) async-start(), calls=%async_computation.4 | async-start | bytes 2359296 | tf_op jit(solution)/shard_map/all_gather | solution.py:61
  377.3 1.3 copy-start.3
  379.3 113.2 %all-gather.16.cloned.1.call-start = ((), (), s32[]{:S(2)}) async-start(), calls=%async_computation.5 | async-start | bytes 8912896 | tf_op jit(solution)/shard_map/all_gather | solution.py:68
  432.7 579.6 %all-gather.20.cloned.1.call-start = ((), (), s32[]{:S(2)}) async-start(), calls=%async_computation.7 | async-start | bytes 35651584 | tf_op jit(solution)/shard_map/all_gather | solution.py:15
  507.2 1.9 copy-start.2
  820.9 2.1 copy-start.5
  842.0 343.6 %all-gather.18.cloned.1.call-start = ((), (), s32[]{:S(2)}) async-start(), calls=%async_computation.6 | async-start | bytes 35651584 | tf_op jit(solution)/shard_map/all_gather | solution.py:15
  1199.1 2.9 copy-start.4
  1207.9 2.0 copy-start.1
Sparse Core Ops, SparseCore 0:
  9.7 73.9 all-gather.7
  116.9 70.3 all-gather.9
  200.9 58.7 all-gather.11
  379.4 51.3 all-gather.13
  432.9 59.6 all-gather.15
  842.1 170.1 all-gather.19
  1014.0 171.6 all-gather.17
